TPU v7x, 32 devices: a whole 2x2x4 slice. The times are simulated.
32 devices in a mesh: rep: 4 (over y, x), shard: 8 (over z, core).
Axes of the slice: x: 2, y: 2, z: 4, core: 2. Of those that a mesh axis runs over, the one named last changes fastest.
Arguments:
- bag_ids: int32 [2048, 20], P(('rep', 'shard')), may hold values from 0 to 4095
- table: float32 [4096, 256], P('shard'), may hold values from -1.2 to 1.2
- accum: float32 [4096], P('shard'), may hold values from 0.01 to 0.1
- cross_weight: float32 [256, 256], replicated, may hold values from -0.375 to 0.375
- cross_bias: float32 [256], replicated, may hold values from -4 to 4
- upstream: float32 [2048, 256], P(('rep', 'shard')), may hold values from -6 to 6
Outputs:
- crossed: float32 [2048, 256], P(('rep', 'shard'))
- new_table: float32 [4096, 256], P('shard')
- new_accum: float32 [4096], P('shard')
All inputs are finite; a program needn't handle non-finite values.
Results may differ from a plain program's by a relative error of at most 0.00014.
Values sent between devices are 32-bit elements; how exact they have to be, the bound alone decides.
A program may use at most 64 MiB of HBM per device.

v0:
```python
import jax
import jax.numpy as jnp
from jax import lax
from jax.sharding import PartitionSpec as P


def adagrad_rows(rows, sums, grads):
    fresh = sums + jnp.mean(grads * grads, axis=1)
    return (rows - 0.5 * grads / jnp.sqrt(fresh)[:, None], fresh)


def count_block(spill_ids, count, rows_owned):
    sample_pos = lax.broadcasted_iota(jnp.int32, spill_ids.shape, 0)
    flat_index = (sample_pos * (rows_owned + 1) + spill_ids).reshape(-1)
    ones_flat = jnp.ones(flat_index.shape, jnp.float32)
    counted = jax.ops.segment_sum(ones_flat, flat_index, num_segments=count * (rows_owned + 1))
    return counted.reshape(count, rows_owned + 1)[:, :rows_owned]


def body(bag_ids, table, accum, cross_weight, cross_bias, upstream):
    per_device = bag_ids.shape[0]
    rows_owned = table.shape[0]
    first_row = lax.axis_index("shard") * rows_owned
    group_ids = lax.all_gather(bag_ids, "shard", axis=0, tiled=True)
    local_ids = group_ids - first_row
    owned = (local_ids >= 0) & (local_ids < rows_owned)
    spill_ids = jnp.where(owned, local_ids, rows_owned)
    counts = count_block(spill_ids, lax.axis_size("shard") * per_device, rows_owned)
    pooled = lax.psum_scatter(
        jnp.dot(counts, table, precision=lax.Precision.HIGHEST),
        "shard",
        scatter_dimension=0,
        tiled=True,
    )
    mixed = jnp.dot(pooled, cross_weight, precision=lax.Precision.HIGHEST) + cross_bias
    crossed = pooled * mixed + pooled
    back = (
        upstream * mixed
        + jnp.dot(upstream * pooled, cross_weight.T, precision=lax.Precision.HIGHEST)
        + upstream
    )
    piece = lax.all_gather(back, "shard", axis=0, tiled=True)
    counts = count_block(spill_ids, piece.shape[0], rows_owned)
    added = lax.dot_general(
        counts, piece, (((0,), (0,)), ((), ())), precision=lax.Precision.HIGHEST
    )
    totals = lax.psum(added, "rep")
    new_table, new_accum = adagrad_rows(table, accum, totals)
    return (crossed, new_table, new_accum)


def solution(mesh):
    placed = (
        P(("rep", "shard"), None),
        P("shard", None),
        P("shard"),
        P(),
        P(),
        P(("rep", "shard"), None),
    )
    return jax.shard_map(
        body,
        mesh=mesh,
        in_specs=placed,
        out_specs=(P(("rep", "shard"), None), P("shard", None), P("shard")),
        check_vma=False,
    )
```

profile of v0, /device:TPU:0, one launch (start us, length us, event | category | flops | bytes accessed | tf_op | source)
XLA Modules:
  0.0 201.8 jit_solution(5128494208951309191)
XLA Ops:
  7.2 0.0 copy-start
  7.2 0.0 reduce-scatter.2.cloned.1.call-start
  7.2 15.8 %all-gather = s32[8,64,20]{1,2,0:T(8,128)S(1)} all-gather(s32[1,64,20]{1,2,0:T(8,128)} %bitcast.8), channel_id=1, replica_groups=mesh['rep'=4,'shard'=8] {'shard'}, dimensions={0}, use_global_device_ids=true | all-gather | bytes 46080 | tf_op jit(solution)/shard_map/all_gather | solution.py:24
  23.1 0.1 reshape.25
  23.2 0.1 copy.14
  23.3 0.2 reshape.15
  23.5 68.7 %scatter_custom_fusion = f32[262656]{0:T(1024)S(1)} fusion(s32[10240]{0:T(1024)S(1)} %reshape.15, f32[10240]{0:T(1024)S(1)} %broadcast.17, f32[]{:T(128)} %constant.8.clone.1), kind=kCustom, calls=%fused_computation.8 | custom fusion | flops 10240 | bytes 1050628 | tf_op jit(solution)/shard_map/scatter-add | solution.py:16
  92.2 0.0 copy-start.1
  92.2 1.0 reshape.12
  93.2 0.1 copy-done.1
  93.3 0.0 copy-start.4
  93.3 0.0 copy-start.2
  93.3 1.8 fusion.3
  95.0 0.0 reduce-scatter.2.cloned.1.call-update
  95.1 0.0 all-reduce.2.cloned.1.call-start
  95.1 31.7 %reduce-scatter.2.cloned.1.call-done = f32[64,256]{1,0:T(8,128)} async-done(((f32[512,256]{1,0:T(8,128)}), f32[64,256]{1,0:T(8,128)}) %reduce-scatter.2.cloned.1.call-update) | async-done | bytes 65552 | tf_op jit(solution)/shard_map/reduce_scatter | solution.py:29
  126.8 0.0 copy-done
  126.8 0.0 copy-done.4
  126.8 1.8 multiply_add_fusion
  128.6 0.0 copy-done.2
  128.6 1.2 fusion
  129.8 15.0 %all_gather.7 = f32[512,256]{1,0:T(8,128)S(1)} all-gather(f32[64,256]{1,0:T(8,128)S(1)} %fusion), channel_id=1, replica_groups=mesh['rep'=4,'shard'=8] {'shard'}, dimensions={0}, use_global_device_ids=true | all-gather | bytes 589824 | tf_op jit(solution)/shard_map/all_gather | solution.py:42
  144.8 0.0 copy-start.3
  144.8 2.6 %fusion.1 = f32[512,256]{1,0:T(8,128)} fusion(f32[512,256]{1,0:T(8,128)S(1)} %all_gather.7, f32[512,513]{1,0:T(8,128)S(1)} %reshape.12), kind=kOutput, calls=%fused_computation.4 | convolution fusion | flops 805306368 | bytes 2097152 | tf_op jit(solution)/shard_map/dot_general | solution.py:44
  147.4 0.0 all-reduce.2.cloned.1.call-update
  147.4 43.8 %all-reduce.2.cloned.1.call-done = f32[512,256]{1,0:T(8,128)} async-done(((f32[512,256]{1,0:T(8,128)}), f32[512,256]{1,0:T(8,128)}) %all-reduce.2.cloned.1.call-update) | async-done | bytes 524304 | tf_op jit(solution)/shard_map/psum | solution.py:47
  191.2 1.2 multiply_reduce_fusion
  192.4 0.0 copy-done.3
  192.4 0.6 fusion.8
  193.0 2.0 divide_subtract_fusion
  (4 shorter events, 0.0 us)
Async XLA Ops:
  7.2 119.6 %copy-start = (f32[256,256]{1,0:T(8,128)S(1)}, f32[256,256]{1,0:T(8,128)}, u32[]{:S(2)}) copy-start(f32[256,256]{1,0:T(8,128)} %param.9) | copy-start | bytes 786436
  7.2 119.6 %reduce-scatter.2.cloned.1.call-start = ((), (), s32[]{:S(2)}) async-start(), calls=%async_computation.1 | async-start | bytes 589824 | tf_op jit(solution)/shard_map/reduce_scatter | solution.py:29
  92.2 1.0 copy-start.1
  93.3 33.5 %copy-start.4 = (f32[256]{0:T(256)S(1)}, f32[256]{0:T(256)}, u32[]{:S(2)}) copy-start(f32[256]{0:T(256)} %param.10) | copy-start | bytes 3076
  93.3 35.3 %copy-start.2 = (f32[64,256]{1,0:T(8,128)S(1)}, f32[64,256]{1,0:T(8,128)}, u32[]{:S(2)}) copy-start(f32[64,256]{1,0:T(8,128)} %param.11) | copy-start | bytes 196612
  95.1 96.2 %all-reduce.2.cloned.1.call-start = ((), (), s32[]{:S(2)}) async-start(), calls=%async_computation.2 | async-start | bytes 1048576 | tf_op jit(solution)/shard_map/psum | solution.py:47
  144.8 47.6 %copy-start.3 = (f32[512]{0:T(512)S(1)}, f32[512]{0:T(512)}, u32[]{:S(2)}) copy-start(f32[512]{0:T(512)} %param.8) | copy-start | bytes 6148
Sparse Core Ops, SparseCore 0:
  95.2 31.5 reduce-scatter.1
  147.6 43.6 all-reduce.1
where the time goes:
time: 202 us
  waiting for transfers between devices  75.5 us (37%)
  other arithmetic  72.5 us (36%)
  blocking collectives  30.8 us (15%)
  between operations  14.1 us (7%)
  matrix products  7.39 us (4%)
    scatter-add x1, other arithmetic, count_block(): jax.ops.segment_sum(ones_flat, flat_index, num_segments=count * (rows_own...  68.7 us
    psum x1, waiting for transfers between devices, body(): totals = lax.psum(added, 'rep')  43.8 us
    reduce_scatter x1, waiting for transfers between devices, body(): lax.psum_scatter(jnp.dot(counts, table, precision=lax.Precision.HIGHEST),...  31.7 us
    all_gather x1, blocking collectives, body(): group_ids = lax.all_gather(bag_ids, 'shard', axis=0, tiled=True)  15.8 us
    all_gather x1, blocking collectives, body(): piece = lax.all_gather(back, 'shard', axis=0, tiled=True)  15 us
  transfers between devices with their start and end apart: 2, of which 2 were waited for; matrix products, arithmetic and copies ran while one was open for 0% of the time, Pallas kernels for 0%

commit v1 on v0

v1 whole, which is shorter than its diff:
```python
import jax
import jax.numpy as jnp
from jax import lax
from jax.experimental import pallas as pl
from jax.experimental.pallas import tpu as pltpu
from jax.sharding import PartitionSpec as P

F32 = jnp.float32
BF16 = jnp.bfloat16
MESH = pl.DeviceIdType.MESH
PLANE = 4
LINE = 4
CHUNK = 256


def split(x):
    hi = x.astype(BF16)
    return hi, (x - hi.astype(F32)).astype(BF16)


def dot(a, b, dims=((1,), (0,))):
    return lax.dot_general(a, b, (dims, ((), ())), preferred_element_type=F32)


def dot3(a, b, dims):
    ah, al = split(a)
    bh, bl = split(b)
    return dot(ah, bh, dims) + (dot(ah, bl, dims) + dot(al, bh, dims))


def kernel(
    bag, ids_ref, table_hbm, accum_ref, weight_ref, bias_ref, up_ref,
    crossed_ref, newt_ref, newa_ref,
    tab, thi, tlo, ids, ct, psend, precv, back, g, grecv,
    load_sem, tab_sem, idz_sem, idp_sem, p_sem, bz_sem, bp_sem, bd_sem, g_sem,
):
    rep = lax.axis_index("rep")
    shard = lax.axis_index("shard")
    z = shard // 2
    core = shard % 2
    rows = tab.shape[1]
    each = up_ref.shape[0]
    mate = (rep, shard + 1 - 2 * core)
    xn = (rep + 1 - 2 * (rep % 2), shard)
    yn = ((rep + 2) % 4, shard)

    def along(k):
        return (rep, ((z + k) % LINE) * 2 + core)

    def send(src, dst, sems, to):
        cp = pltpu.make_async_remote_copy(
            src_ref=src, dst_ref=dst, send_sem=sems.at[0], recv_sem=sems.at[1],
            device_id=to, device_id_type=MESH,
        )
        cp.start()
        return cp

    load = pltpu.make_async_copy(table_hbm, tab.at[0], load_sem)
    load.start()
    ids[0, 0] = ids_ref[...]

    barrier = pltpu.get_barrier_semaphore()
    for to in (mate, xn, yn, along(1), along(2), along(3)):
        pl.semaphore_signal(barrier, inc=1, device_id=to, device_id_type=MESH)
    pl.semaphore_wait(barrier, 6)

    sent = []
    idz = [send(ids_ref, ids.at[0, j], idz_sem.at[j - 1], along(j)) for j in (1, 2, 3)]
    tcp = send(table_hbm, tab.at[1], tab_sem, mate)
    load.wait()
    hi, lo = split(tab[0])
    thi[0:rows] = hi
    tlo[0:rows] = lo
    for cp in idz:
        cp.wait()
    idx = send(ids.at[0], ids.at[1], idp_sem.at[0], xn)
    idy = send(ids.at[0], ids.at[2], idp_sem.at[1], yn)

    own_first = shard * rows
    mate_first = (shard + 1 - 2 * core) * rows
    per_block = rows // CHUNK
    row16 = lax.broadcasted_iota(jnp.int32, (CHUNK, 128), 0).astype(F32).astype(BF16)
    lane = lax.broadcasted_iota(jnp.int32, ids.shape[2:], 1)

    def count(r, p):
        pair = jnp.where(lane < each, ids[r, 2 * p], ids[r, 2 * p + 1])

        def step(q, carry):
            base = jnp.where(q < per_block, own_first, mate_first) + (q % per_block) * CHUNK
            local = pair - base
            local = jnp.where((local >= 0) & (local < CHUNK), local, -1).astype(F32)
            acc = jnp.zeros((CHUNK, 128), BF16)
            for j in range(bag):
                one = jnp.broadcast_to(local[j : j + 1], (16, 128)).astype(BF16)
                wide = jnp.concatenate([one] * (CHUNK // 16), axis=0)
                acc = acc + jnp.where(wide == row16, jnp.ones_like(acc), jnp.zeros_like(acc))
            ct[r, pl.ds(pl.multiple_of(q * CHUNK, CHUNK), CHUNK), pl.ds(p * 128, 128)] = acc
            return carry

        lax.fori_loop(0, 2 * per_block, step, 0)

    count(0, 1)
    count(0, 0)
    tcp.wait()
    hi, lo = split(tab[1])
    thi[rows : 2 * rows] = hi
    tlo[rows : 2 * rows] = lo
    pcp = []
    mine = None
    for p in (1, 0):
        c = ct[0, :, p * 128 : (p + 1) * 128]
        part = dot(c, thi[...], ((0,), (0,))) + dot(c, tlo[...], ((0,), (0,)))
        for h in (0, 1):
            j = 2 * p + h
            block = part[h * each : (h + 1) * each]
            if j == 0:
                mine = block
            else:
                psend[j - 1] = block
                pcp.append(send(psend.at[j - 1], precv.at[j - 1], p_sem.at[j - 1], along(LINE - j)))

    idx.wait()
    idd = send(ids.at[1], ids.at[3], idp_sem.at[2], yn)
    count(1, 0)
    count(1, 1)
    idy.wait()
    count(2, 0)
    count(2, 1)
    idd.wait()
    count(3, 0)
    count(3, 1)

    for cp in pcp:
        cp.wait()
    pooled = (mine + precv[0]) + (precv[1] + precv[2])
    weight = weight_ref[...]
    up = up_ref[...]
    mixed = dot3(pooled, weight, ((1,), (0,))) + bias_ref[...]
    own_back = up * mixed + dot3(up * pooled, weight, ((1,), (1,))) + up
    back[0, 0:each] = own_back

    half = each // 2

    def block(r, j, start=0, size=each):
        return back.at[r, pl.ds(j * each + start, size)]

    zcp = {j: send(block(0, 0), block(0, j), bz_sem.at[j - 1], along(j)) for j in (1, 2, 3)}
    xcp, ycp, dx, dy = {}, {}, {}, {}

    def forward(j):
        xcp[j] = send(block(0, j), block(1, j), bp_sem.at[0, j], xn)
        ycp[j] = send(block(0, j), block(2, j), bp_sem.at[1, j], yn)

    def diagonal(j):
        xcp[j].wait_recv()
        dy[j] = send(block(1, j, 0, half), block(3, j, 0, half), bd_sem.at[0, j], yn)
        ycp[j].wait_recv()
        dx[j] = send(block(2, j, half, half), block(3, j, half, half), bd_sem.at[1, j], xn)

    def product(r):
        bh, bl = split(back[r])
        g[r] = dot(ct[r], bh) + dot(ct[r], bl)

    forward(0)
    crossed_ref[...] = pooled * mixed + pooled
    for j in (1, 2, 3):
        zcp[j].wait_recv()
        forward(j)
        diagonal(j - 1)
    diagonal(3)
    product(0)
    product(1)
    product(2)
    for j in range(LINE):
        dy[j].wait_recv()
        dx[j].wait_recv()
    product(3)
    g[0] = (g[0] + g[1]) + (g[2] + g[3])
    gcp = send(g.at[0, pl.ds(rows, rows)], grecv, g_sem, mate)
    for d in (zcp, xcp, ycp, dx, dy):
        for cp in d.values():
            cp.wait_send()
    gcp.wait()
    total = g[0, 0:rows] + grecv[...]
    mean = jnp.sum(total * total, axis=1, keepdims=True) * (1.0 / total.shape[1])
    acc_col = jnp.transpose(jnp.broadcast_to(accum_ref[...], (8, rows)))[:, 0:1]
    fresh = acc_col + mean
    newt_ref[...] = tab[0] - 0.5 * total * lax.rsqrt(fresh)
    newa_ref[...] = jnp.transpose(jnp.broadcast_to(fresh, (rows, 128)))[0:1]


def fused_body(bag_ids, table, accum, cross_weight, cross_bias, upstream):
    each, bag = bag_ids.shape
    rows, width = table.shape
    tall = -(-bag // 8) * 8
    ids = jnp.pad(bag_ids.T, ((0, tall - bag), (0, 0)), constant_values=-1)
    ids = jnp.concatenate([ids, ids], axis=1)
    vmem = pl.BlockSpec(memory_space=pltpu.VMEM)
    dma = pltpu.SemaphoreType.DMA
    crossed, new_table, new_accum = pl.pallas_call(
        lambda *refs: kernel(bag, *refs),
        out_shape=(
            jax.ShapeDtypeStruct((each, width), F32),
            jax.ShapeDtypeStruct((rows, width), F32),
            jax.ShapeDtypeStruct((1, rows), F32),
        ),
        in_specs=[vmem, pl.BlockSpec(memory_space=pl.ANY), vmem, vmem, vmem, vmem],
        out_specs=(vmem, vmem, vmem),
        scratch_shapes=[
            pltpu.VMEM((2, rows, width), F32),
            pltpu.VMEM((2 * rows, width), BF16),
            pltpu.VMEM((2 * rows, width), BF16),
            pltpu.VMEM((PLANE, LINE, tall, 128), jnp.int32),
            pltpu.VMEM((PLANE, 2 * rows, LINE * each), BF16),
            pltpu.VMEM((LINE - 1, each, width), F32),
            pltpu.VMEM((LINE - 1, each, width), F32),
            pltpu.VMEM((PLANE, LINE * each, width), F32),
            pltpu.VMEM((PLANE, 2 * rows, width), F32),
            pltpu.VMEM((rows, width), F32),
            dma,
            dma((2,)),
            dma((3, 2)),
            dma((3, 2)),
            dma((3, 2)),
            dma((3, 2)),
            dma((2, LINE, 2)),
            dma((2, LINE, 2)),
            dma((2,)),
        ],
        compiler_params=pltpu.CompilerParams(
            collective_id=0, has_side_effects=True, vmem_limit_bytes=40 * 1024 * 1024
        ),
    )(ids, table, accum.reshape(1, rows), cross_weight, cross_bias.reshape(1, width), upstream)
    return crossed, new_table, new_accum.reshape(rows)


def adagrad_rows(rows, sums, grads):
    fresh = sums + jnp.mean(grads * grads, axis=1)
    return (rows - 0.5 * grads / jnp.sqrt(fresh)[:, None], fresh)


def general_body(bag_ids, table, accum, cross_weight, cross_bias, upstream):
    rows_owned = table.shape[0]
    first_row = lax.axis_index("shard") * rows_owned
    group_ids = lax.all_gather(bag_ids, "shard", axis=0, tiled=True)
    local = group_ids - first_row
    number = lax.broadcasted_iota(jnp.int32, (1, rows_owned), 1)
    counts = jnp.zeros((local.shape[0], rows_owned), F32)
    for j in range(local.shape[1]):
        counts = counts + (local[:, j : j + 1] == number).astype(F32)
    pooled = lax.psum_scatter(
        jnp.dot(counts, table, precision=lax.Precision.HIGHEST),
        "shard",
        scatter_dimension=0,
        tiled=True,
    )
    mixed = jnp.dot(pooled, cross_weight, precision=lax.Precision.HIGHEST) + cross_bias
    crossed = pooled * mixed + pooled
    back = (
        upstream * mixed
        + jnp.dot(upstream * pooled, cross_weight.T, precision=lax.Precision.HIGHEST)
        + upstream
    )
    piece = lax.all_gather(back, "shard", axis=0, tiled=True)
    added = lax.dot_general(
        counts, piece, (((0,), (0,)), ((), ())), precision=lax.Precision.HIGHEST
    )
    totals = lax.psum(added, "rep")
    new_table, new_accum = adagrad_rows(table, accum, totals)
    return (crossed, new_table, new_accum)


def solution(mesh):
    placed = (
        P(("rep", "shard"), None),
        P("shard", None),
        P("shard"),
        P(),
        P(),
        P(("rep", "shard"), None),
    )
    small = mesh.shape["rep"] == PLANE and mesh.shape["shard"] == 2 * LINE
    return jax.shard_map(
        fused_body if small else general_body,
        mesh=mesh,
        in_specs=placed,
        out_specs=(P(("rep", "shard"), None), P("shard", None), P("shard")),
        check_vma=False,
    )
```

time: 202 us -> 42.3 us (0.21)
  waiting for transfers between devices: 75.5 us -> 0 us
  other arithmetic: 72.5 us -> 0.08 us
  Pallas kernels: 0 us -> 35.1 us
  blocking collectives: 30.8 us -> 0 us
  between operations: 14.1 us -> 0.65 us
  matrix products: 7.39 us -> 0 us
  local copies, waits for them, and re-layouts: 1.46 us -> 6.16 us
    scatter-add x1 -> x0, other arithmetic: 68.7 us -> none  [count_block(): jax.ops.segment_sum(ones_flat, flat_index, num_segments=count * (rows_own...]
    psum x1 -> x0, waiting for transfers between devices: 43.8 us -> none  [body(): totals = lax.psum(added, 'rep')]
    pallas_call x0 -> x1, Pallas kernels: none -> 35.1 us  [fused_body(): pl.pallas_call(lambda *refs: kernel(bag, *refs), out_shape=(jax.ShapeDtyp...]
    reduce_scatter x1 -> x0, waiting for transfers between devices: 31.7 us -> none  [body(): lax.psum_scatter(jnp.dot(counts, table, precision=lax.Precision.HIGHEST),...]
    all_gather x2 -> x0, blocking collectives: 30.8 us -> none  [the longest x1 15.8 us: body(): group_ids = lax.all_gather(bag_ids, 'shard', axis=0, tiled=True)]
    dot_general x4 -> x0, matrix products: 7.39 us -> none  [the longest x1 2.6 us: body(): lax.dot_general(counts, piece, (((0,), (0,)), ((), ())), precision=lax.Pr...]
    unnamed x10 -> x13, local copies, waits for them, and re-layouts: 0.09 us -> 5.45 us
  transfers between devices with their start and end apart: 2 -> 0, of which waited for: 2 -> 0; matrix products, arithmetic and copies ran while one was open for 0% -> 0% of each run, Pallas kernels for 0% -> 0%
where the time goes in v1:
time: 42.3 us; the launch traced here: 42 us
  Pallas kernels  35.1 us (83%)
  local copies, waits for them, and re-layouts  6.16 us (15%)
  between operations  0.65 us (2%)
    pallas_call x1, Pallas kernels, fused_body(): pl.pallas_call(lambda *refs: kernel(bag, *refs), out_shape=(jax.ShapeDtyp...  35.1 us
    unnamed x13, local copies, waits for them, and re-layouts  5.45 us

profile of v1, /device:TPU:0, one launch (start us, length us, event | category | flops | bytes accessed | tf_op | source)
XLA Modules:
  0.0 42.0 jit_solution(8317208625044565017)
XLA Ops:
  0.6 0.7 %pad.4 = s32[24,64]{1,0:T(8,128)S(1)} pad(s32[20,64]{1,0:T(8,128)} %bitcast.7, s32[]{:T(128)} %constant.0.clone.1), padding=0_4x0_0 | pad | bytes 11268 | tf_op jit(solution)/shard_map/jit(_pad)/pad | solution.py:196
  1.3 0.0 copy-start.3
  1.3 0.0 copy-start.4
  1.4 0.1 pad_add_fusion.refs_0_
  1.4 0.6 %copy-done.3 = f32[512]{0:T(512)S(1)} copy-done((f32[512]{0:T(512)S(1)}, f32[512]{0:T(512)}, u32[]{:S(2)}) %copy-start.3) | copy-done | bytes 2072
  2.0 0.0 copy-done.4
  2.0 0.0 copy-start
  2.0 1.0 %copy-done = f32[512,256]{1,0:T(8,128)S(1)} copy-done((f32[512,256]{1,0:T(8,128)S(1)}, f32[512,256]{1,0:T(8,128)}, u32[]{:S(2)}) %copy-start) | copy-done | bytes 524312
  3.1 0.0 copy-start.1
  3.1 0.9 %copy-done.1 = f32[256,256]{1,0:T(8,128)S(1)} copy-done((f32[256,256]{1,0:T(8,128)S(1)}, f32[256,256]{1,0:T(8,128)}, u32[]{:S(2)}) %copy-start.1) | copy-done | bytes 262168
  4.0 0.0 copy-start.2
  4.0 0.8 %copy-done.2 = f32[64,256]{1,0:T(8,128)S(1)} copy-done((f32[64,256]{1,0:T(8,128)S(1)}, f32[64,256]{1,0:T(8,128)}, u32[]{:S(2)}) %copy-start.2) | copy-done | bytes 65560
  4.9 35.1 %shard_map.85 = (f32[64,256]{1,0:T(8,128)S(1)}, f32[512,256]{1,0:T(8,128)S(1)}, f32[1,512]{1,0:T(1,128)S(1)}) custom-call(s32[24,128]{1,0:T(8,128)S(1)} %pad_add_fusion.refs_0_, f32[512,256]{1,0:T(8,128)S(1)} %copy-done, f32[1,512]{1,0:T(1,128)S(1)} %bitcast.4, f32[256,256]{1,0:T(8,128)S(1)} %copy-done.1, f32[1,256]{1,0:T(1,128)S(1)} %bitcast.6, ...), custom_call_target="tpu_custom_call" | custom-call | tf_op jit(solution)/shard_map/pallas_call | solution.py:200
  40.0 0.6 %copy.12 = f32[64,256]{1,0:T(8,128)} copy(f32[64,256]{1,0:T(8,128)S(1)} %get-tuple-element.12) | data formatting | bytes 131072
  40.6 0.8 %copy.13 = f32[512,256]{1,0:T(8,128)} copy(f32[512,256]{1,0:T(8,128)S(1)} %get-tuple-element.13) | data formatting | bytes 1048576
  41.4 0.6 %copy.14 = f32[512]{0:T(512)} copy(f32[512]{0:T(512)S(1)} %bitcast.5) | data formatting | bytes 4096
Async XLA Ops:
  1.3 0.7 %copy-start.3 = (f32[512]{0:T(512)S(1)}, f32[512]{0:T(512)}, u32[]{:S(2)}) copy-start(f32[512]{0:T(512)} %param.8) | copy-start | bytes 6148
  1.3 0.7 %copy-start.4 = (f32[256]{0:T(256)S(1)}, f32[256]{0:T(256)}, u32[]{:S(2)}) copy-start(f32[256]{0:T(256)} %param.10) | copy-start | bytes 3076
  2.0 1.0 %copy-start = (f32[512,256]{1,0:T(8,128)S(1)}, f32[512,256]{1,0:T(8,128)}, u32[]{:S(2)}) copy-start(f32[512,256]{1,0:T(8,128)} %refs_1_.1) | copy-start | bytes 1572868
  3.1 0.9 %copy-start.1 = (f32[256,256]{1,0:T(8,128)S(1)}, f32[256,256]{1,0:T(8,128)}, u32[]{:S(2)}) copy-start(f32[256,256]{1,0:T(8,128)} %refs_3_.1) | copy-start | bytes 786436
  4.0 0.8 %copy-start.2 = (f32[64,256]{1,0:T(8,128)S(1)}, f32[64,256]{1,0:T(8,128)}, u32[]{:S(2)}) copy-start(f32[64,256]{1,0:T(8,128)} %refs_5_.1) | copy-start | bytes 196612
